TPU v7x, 32 devices: a whole 2x2x4 slice. The times are simulated.
32 devices in a mesh: freq: 8 (over z, x), rec: 4 (over y, core).
Axes of the slice: x: 2, y: 2, z: 4, core: 2. Of those that a mesh axis runs over, the one named last changes fastest.
Arguments:
- response: float32 [2, 128, 1024, 1024], P(None, 'freq', 'rec'), may hold values from -0.1875 to 0.1875
- focus_plus: float32 [2, 128, 1024, 64], P(None, 'freq', 'rec'), may hold values from -6 to 6
- direct: float32 [2, 128, 1024, 64], P(None, 'freq', 'rec'), may hold values from -6 to 6
- onset: int32 [1024, 64], P('rec'), may hold values from 4 to 64
Outputs:
- focus_minus: float32 [2, 128, 1024, 64], P(None, 'freq', 'rec')
- focus_plus_next: float32 [2, 128, 1024, 64], P(None, 'freq', 'rec')
All inputs are finite; a program needn't handle non-finite values.
Results may differ from a plain program's by a relative error of at most 0.00007.
Values sent between devices are 32-bit elements; how exact they have to be, the bound alone decides.
A program may use at most 192 MiB of HBM per device.

v0:
```python
import math

import jax
import jax.numpy as jnp
from jax import lax
from jax.sharding import PartitionSpec as P


def full_einsum(form, left, right):
    return jnp.einsum(form, left, right, precision=lax.Precision.HIGHEST)


def make_tables(freq_total):
    counter = jnp.arange(freq_total, dtype=jnp.int32)
    phase_steps = counter[:, None] * counter[None, :] % freq_total
    phase_angle = phase_steps.astype(jnp.float32) * (2.0 * math.pi / freq_total)
    cosine = jnp.cos(phase_angle)
    sine_table = jnp.sin(phase_angle)
    inverse = (
        jnp.concatenate(
            [jnp.concatenate([cosine, -sine_table], 1), jnp.concatenate([sine_table, cosine], 1)], 0
        )
        / freq_total
    )
    forward = jnp.concatenate(
        [jnp.concatenate([cosine, sine_table], 1), jnp.concatenate([-sine_table, cosine], 1)], 0
    )
    return (inverse, forward)


def windowed(traces, onset_flat, inverse, forward):
    freq_total = traces.shape[1]
    stacked = traces.reshape(2 * freq_total, -1)
    time_traces = jnp.dot(inverse, stacked, precision=lax.Precision.HIGHEST)
    counter = jnp.arange(freq_total, dtype=jnp.int32)
    distance = jnp.minimum(counter, freq_total - counter)
    window_mask = (distance[:, None] < onset_flat[None, :]).astype(jnp.float32)
    window_mask = jnp.concatenate([window_mask, window_mask], 0)
    spectra = jnp.dot(forward, time_traces * window_mask, precision=lax.Precision.HIGHEST)
    return spectra.reshape(traces.shape)


def per_device(response, focus_plus, direct, onset):
    freq_dev = response.shape[1]
    row_count = response.shape[2]
    focal_count = focus_plus.shape[3]
    groups = lax.axis_size("freq")
    freq_index = lax.axis_index("freq")
    flat_count = row_count * focal_count
    piece_len = flat_count // groups
    local_onset = lax.dynamic_slice_in_dim(onset.reshape(-1), freq_index * piece_len, piece_len, 0)
    inverse, forward = make_tables(freq_dev * groups)
    shard_piece = lax.all_gather(focus_plus, "rec", axis=2, tiled=True)
    real_block = response[0]
    imag_block = response[1]
    joined = jnp.concatenate([shard_piece[0], shard_piece[1]], axis=2)
    from_real = full_einsum("wrs,wsf->wrf", real_block, joined)
    from_imag = full_einsum("wrs,wsf->wrf", imag_block, joined)
    new_real = from_real[:, :, :focal_count] - from_imag[:, :, focal_count:]
    new_imag = from_real[:, :, focal_count:] + from_imag[:, :, :focal_count]
    spectra = jnp.stack([new_real, new_imag]).reshape(2, freq_dev, flat_count)
    in_time = lax.all_to_all(spectra, "freq", split_axis=2, concat_axis=1, tiled=True)
    filtered = windowed(in_time, local_onset, inverse, forward)
    focus_minus = lax.all_to_all(filtered, "freq", split_axis=1, concat_axis=2, tiled=True).reshape(
        2, freq_dev, row_count, focal_count
    )
    minus_joined = jnp.concatenate([focus_minus[0], focus_minus[1]], axis=2)
    real_block = response[0]
    imag_block = response[1]
    from_real = full_einsum("wrs,wrf->swf", real_block, minus_joined)
    from_imag = full_einsum("wrs,wrf->swf", imag_block, minus_joined)
    h_real = from_real[:, :, :focal_count] + from_imag[:, :, focal_count:]
    h_imag = from_real[:, :, focal_count:] - from_imag[:, :, :focal_count]
    summed = lax.psum_scatter(
        jnp.stack([h_real, h_imag], axis=1), "rec", scatter_dimension=0, tiled=True
    )
    arranged_sum = jnp.transpose(summed, (1, 2, 0, 3)).reshape(2, freq_dev, flat_count)
    arranged = lax.all_to_all(arranged_sum, "freq", split_axis=2, concat_axis=1, tiled=True)
    windowed_back = windowed(arranged, local_onset, inverse, forward)
    returned = lax.all_to_all(
        windowed_back, "freq", split_axis=1, concat_axis=2, tiled=True
    ).reshape(2, freq_dev, row_count, focal_count)
    return (focus_minus, direct + returned)


def solution(mesh):
    placed = (
        P(None, "freq", "rec", None),
        P(None, "freq", "rec", None),
        P(None, "freq", "rec", None),
        P("rec", None),
    )
    return jax.shard_map(
        per_device,
        mesh=mesh,
        in_specs=placed,
        out_specs=(P(None, "freq", "rec", None), P(None, "freq", "rec", None)),
        check_vma=False,
    )
```

profile of v0, /device:TPU:15, one launch (start us, length us, event | category | flops | bytes accessed | tf_op | source)
XLA Modules:
  0.0 706.9 jit_solution(4838996889746736755)
XLA Ops:
  7.9 60.6 %all-gather.2.cloned.1.call-done = f32[2,16,1024,64]{2,3,1,0:T(8,128)} async-done(((f32[2,16,256,64]{2,3,1,0:T(8,128)}), f32[2,16,1024,64]{2,3,1,0:T(8,128)}) %all-gather.2.cloned.1.call-update) | async-done | bytes 8388624 | tf_op jit(solution)/shard_map/all_gather | solution.py:53
  73.6 20.2 %fusion.20 = f32[16,256,128]{1,2,0:T(8,128)S(1)} fusion(f32[2,16,256,1024]{3,2,1,0:T(8,128)} %param.4, f32[16,1024,64]{1,2,0:T(8,128)S(1)} %get-tuple-element.13, f32[16,1024,64]{1,2,0:T(8,128)S(1)} %get-tuple-element.12), kind=kOutput, calls=%fused_computation.27 | convolution fusion | flops 6444548096 | bytes 27262976 | tf_op jit(solution)/shard_map/wrs,wsf->wrf/dot_general | solution.py:10
  93.8 20.4 %fusion.23 = f32[16,256,128]{1,2,0:T(8,128)S(1)} fusion(f32[2,16,256,1024]{3,2,1,0:T(8,128)} %param.4, f32[16,1024,64]{1,2,0:T(8,128)S(1)} %get-tuple-element.13, f32[16,1024,64]{1,2,0:T(8,128)S(1)} %get-tuple-element.12), kind=kOutput, calls=%fused_computation.28 | convolution fusion | flops 6444548096 | bytes 27262976 | tf_op jit(solution)/shard_map/wrs,wsf->wrf/dot_general | solution.py:10
  123.0 14.8 %copy.54 = f32[2,16,16384]{1,0,2:T(2,128)} copy(f32[2,16,16384]{2,1,0:T(8,128)S(1)} %pad_maximum_fusion.4) | data formatting | bytes 4194304 | tf_op jit(solution)/shard_map/stack | solution.py:61
  137.9 24.7 %reshape.56 = f32[8,1,65536]{2,1,0:T(1,128)} reshape(f32[16384,2,16]{2,1,0:T(2,128)} %bitcast.70) | data formatting | bytes 4194304
  169.7 44.2 %all-to-all-done = f32[8,1,65536]{2,1,0:T(1,128)S(1)} async-done(((f32[8,1,65536]{2,1,0:T(1,128)}), f32[8,1,65536]{2,1,0:T(1,128)S(1)}, u32[]{:S(2)}, u32[]{:S(2)}) %all-to-all-start) | async-done | bytes 2097184 | tf_op jit(solution)/shard_map/all_to_all | solution.py:62
  215.7 7.1 %reduce = f32[8,65536]{1,0:T(8,128)S(1)} reduce(f32[8,1,65536]{2,1,0:T(1,128)} %copy-done.1, f32[]{:T(128)} %broadcast.32), dimensions={1}, to_apply=%all_to_all.44.reduce_sub_computation | reduce | bytes 4194308 | tf_op jit(solution)/shard_map/all_to_all | solution.py:62
  222.9 28.4 %reshape.57 = f32[16384,2,16]{2,1,0:T(2,128)} reshape(f32[8,65536]{1,0:T(8,128)S(1)} %reduce) | data formatting | bytes 4194304
  251.3 20.1 %copy.75 = f32[2,16,8,2048]{3,1,2,0:T(8,128)S(1)} copy(f32[2,16,8,2048]{1,0,3,2:T(2,128)} %bitcast.71) | data formatting | bytes 4194304 | tf_op jit(solution)/shard_map/all_to_all | solution.py:62
  277.0 51.6 %all_to_all.60 = f32[2,128,2048]{2,0,1:T(2,128)S(1)} all-to-all(f32[2,128,2048]{2,0,1:T(2,128)S(1)} %copy.57), channel_id=1, replica_groups=mesh['freq'=8,'rec'=4] {'freq'}, dimensions={1} | all-to-all | bytes 4194304 | tf_op jit(solution)/shard_map/all_to_all | solution.py:64
  344.9 16.1 %fusion.14 = f32[1024,16,128]{0,2,1:T(8,128)} fusion(f32[2,16,256,1024]{3,2,1,0:T(8,128)} %param.4, f32[16,256,64]{1,2,0:T(8,128)} %copy.63, f32[16,256,64]{1,2,0:T(8,128)S(1)} %copy.62), kind=kOutput, calls=%fused_computation.20 | convolution fusion | flops 6442975232 | bytes 27262976 | tf_op jit(solution)/shard_map/wrs,wrf->swf/dot_general | solution.py:10
  361.0 15.6 %fusion.17 = f32[1024,16,128]{0,2,1:T(8,128)} fusion(f32[2,16,256,1024]{3,2,1,0:T(8,128)} %param.4, f32[16,256,64]{1,2,0:T(8,128)S(1)} %copy-done, f32[16,256,64]{1,2,0:T(8,128)S(1)} %copy.62), kind=kOutput, calls=%fused_computation.21 | convolution fusion | flops 6442975232 | bytes 27262976 | tf_op jit(solution)/shard_map/wrs,wrf->swf/dot_general | solution.py:10
  376.6 12.1 %fusion.13 = (f32[1024,1,16,64]{0,3,2,1:T(8,128)}, f32[1024,1,16,64]{0,3,2,1:T(8,128)}) fusion(f32[1024,16,128]{0,2,1:T(8,128)} %fusion.17, f32[1024,16,128]{0,2,1:T(8,128)} %fusion.14), kind=kLoop, calls=%fused_computation.17 | loop fusion | flops 2097152 | bytes 25165824 | tf_op jit(solution)/shard_map/stack | solution.py:75
  388.6 8.4 %pad_maximum_fusion.1 = f32[1024,2,16,64]{0,3,2,1:T(8,128)} fusion(f32[1024,1,16,64]{0,3,2,1:T(8,128)} %get-tuple-element.11, f32[1024,1,16,64]{0,3,2,1:T(8,128)} %get-tuple-element.10), kind=kLoop, calls=%fused_computation.13 | loop fusion | flops 2097152 | bytes 16777216 | tf_op jit(solution)/shard_map/stack | solution.py:75
  397.0 73.0 %reduce-scatter.2.cloned.1.call-done = f32[256,2,16,64]{0,3,2,1:T(8,128)} async-done(((f32[1024,2,16,64]{0,3,2,1:T(8,128)}), f32[256,2,16,64]{0,3,2,1:T(8,128)}) %reduce-scatter.2.cloned.1.call-update) | async-done | bytes 2097168 | tf_op jit(solution)/shard_map/reduce_scatter | solution.py:74
  470.0 14.5 %copy.76 = f32[2,16,256,64]{1,0,3,2:T(2,128)} copy(f32[2,16,256,64]{2,3,1,0:T(8,128)} %bitcast.81) | data formatting | bytes 4194304 | tf_op jit(solution)/shard_map/reshape | solution.py:77
  484.5 24.7 %reshape.58 = f32[8,1,65536]{2,1,0:T(1,128)} reshape(f32[16384,2,16]{2,1,0:T(2,128)} %bitcast.72) | data formatting | bytes 4194304
  509.2 50.8 %all_to_all.61 = f32[8,1,65536]{2,1,0:T(1,128)} all-to-all(f32[8,1,65536]{2,1,0:T(1,128)} %reshape.58), channel_id=1, replica_groups=mesh['freq'=8,'rec'=4] {'freq'}, dimensions={0} | all-to-all | bytes 4194304 | tf_op jit(solution)/shard_map/all_to_all | solution.py:78
  560.0 8.5 %reduce.1 = f32[8,65536]{1,0:T(8,128)} reduce(f32[8,1,65536]{2,1,0:T(1,128)} %all_to_all.61, f32[]{:T(128)} %broadcast.32), dimensions={1}, to_apply=%all_to_all.50.reduce_sub_computation | reduce | bytes 4194308 | tf_op jit(solution)/shard_map/all_to_all | solution.py:78
  568.5 31.8 %reshape.59 = f32[16384,2,16]{2,1,0:T(2,128)} reshape(f32[8,65536]{1,0:T(8,128)} %reduce.1) | data formatting | bytes 4194304
  600.3 21.6 %copy.78 = f32[2,16,8,2048]{3,1,2,0:T(8,128)} copy(f32[2,16,8,2048]{1,0,3,2:T(2,128)} %bitcast.73) | data formatting | bytes 4194304 | tf_op jit(solution)/shard_map/all_to_all | solution.py:78
  630.3 6.8 all-to-all-start.3
  652.1 30.6 %all-to-all-done.3 = f32[2,128,2048]{2,0,1:T(2,128)} async-done(((f32[2,128,2048]{2,0,1:T(2,128)}), f32[2,128,2048]{2,0,1:T(2,128)}, u32[]{:S(2)}, u32[]{:S(2)}) %all-to-all-start.3) | async-done | bytes 2097184 | tf_op jit(solution)/shard_map/all_to_all | solution.py:80
  689.8 6.1 add.38
  (56 shorter events, 79.5 us)
Async XLA Ops:
  7.2 61.3 %all-gather.2.cloned.1.call-start = ((), (), s32[]{:S(2)}) async-start(), calls=%async_computation.5 | async-start | bytes 10485760 | tf_op jit(solution)/shard_map/all_gather | solution.py:53
  117.8 1.6 copy-start.2
  120.0 1.6 copy-start.3
  162.6 6.1 copy-start.6
  162.6 51.3 %all-to-all-start = ((f32[8,1,65536]{2,1,0:T(1,128)}), f32[8,1,65536]{2,1,0:T(1,128)S(1)}, u32[]{:S(2)}, u32[]{:S(2)}) async-start(f32[8,1,65536]{2,1,0:T(1,128)} %reshape.56), calls=%async_computation | async-start | bytes 4194304 | tf_op jit(solution)/shard_map/all_to_all | solution.py:62
  168.2 301.8 %reduce-scatter.2.cloned.1.call-start = ((), (), s32[]{:S(2)}) async-start(), calls=%async_computation.6 | async-start | bytes 10485760 | tf_op jit(solution)/shard_map/reduce_scatter | solution.py:74
  169.4 104.0 %copy-start.4 = (f32[128,128]{1,0:T(8,128)}, f32[128,128]{1,0:T(8,128)S(1)}, u32[]{:S(2)}) copy-start(f32[128,128]{1,0:T(8,128)S(1)} %get-tuple-element.19) | copy-start | bytes 196612
  213.9 1.3 copy-start.1
  344.9 16.1 %copy-start = (f32[16,256,64]{1,2,0:T(8,128)S(1)}, f32[16,256,64]{1,2,0:T(8,128)}, u32[]{:S(2)}) copy-start(f32[16,256,64]{1,2,0:T(8,128)} %copy.63) | copy-start | bytes 3145732
  600.2 21.6 %copy-start.5 = (f32[128,128]{1,0:T(8,128)S(1)}, f32[128,128]{1,0:T(8,128)}, u32[]{:S(2)}) copy-start(f32[128,128]{1,0:T(8,128)} %copy-done.4) | copy-start | bytes 196612
  630.3 52.4 %all-to-all-start.3 = ((f32[2,128,2048]{2,0,1:T(2,128)}), f32[2,128,2048]{2,0,1:T(2,128)}, u32[]{:S(2)}, u32[]{:S(2)}) async-start(f32[2,128,2048]{2,0,1:T(2,128)} %copy.68), calls=%async_computation.4 | async-start | bytes 4194304 | tf_op jit(solution)/shard_map/all_to_all | solution.py:80
Sparse Core Ops, SparseCore 0:
  9.6 58.8 all-gather.1
  397.1 72.8 reduce-scatter.1
where the time goes:
time: 720 us; the launch traced here: 707 us
  local copies, waits for them, and re-layouts  240 us (33%)
  waiting for transfers between devices  209 us (29%)
  blocking collectives  102 us (14%)
  matrix products  81.8 us (11%)
  other arithmetic  45.9 us (6%)
  between operations  14.7 us (2%)
  starting transfers between devices  12.9 us (2%)
    unnamed x22, local copies, waits for them, and re-layouts  122 us
    reduce_scatter x1, waiting for transfers between devices, per_device(): lax.psum_scatter(jnp.stack([h_real, h_imag], axis=1), 'rec', scatter_dime...  73 us
    dot_general x4, matrix products, full_einsum(): return jnp.einsum(form, left, right, precision=lax.Precision.HIGHEST)  72.3 us
    all_gather x1, waiting for transfers between devices, per_device(): shard_piece = lax.all_gather(focus_plus, 'rec', axis=2, tiled=True)  60.6 us
    all_to_all x1, blocking collectives, per_device(): lax.all_to_all(filtered, 'freq', split_axis=1, concat_axis=2, tiled=True)  51.6 us
    all_to_all x1, blocking collectives, per_device(): lax.all_to_all(arranged_sum, 'freq', split_axis=2, concat_axis=1, tiled=T...  50.8 us
    all_to_all x1, waiting for transfers between devices, per_device(): lax.all_to_all(spectra, 'freq', split_axis=2, concat_axis=1, tiled=True)  44.2 us
    all_to_all x1, waiting for transfers between devices, per_device(): lax.all_to_all(windowed_back, 'freq', split_axis=1, concat_axis=2, tiled=...  30.6 us
  transfers between devices with their start and end apart: 4, of which 4 were waited for; matrix products, arithmetic and copies ran while one was open for 2% of the time, Pallas kernels for 0%

commit v1 on v0

--- a/solution.py
+++ b/solution.py
@@ -1,9 +1,18 @@
+import functools
 import math
 
 import jax
 import jax.numpy as jnp
+import ml_dtypes
+import numpy as np
 from jax import lax
+from jax.experimental import pallas as pl
+from jax.experimental.pallas import tpu as pltpu
 from jax.sharding import PartitionSpec as P
+
+MESH = pl.DeviceIdType.MESH
+SLOTS = 4
+TILE = 8
 
 
 def full_einsum(form, left, right):
@@ -40,7 +49,7 @@
     return spectra.reshape(traces.shape)
 
 
-def per_device(response, focus_plus, direct, onset):
+def per_device_general(response, focus_plus, direct, onset):
     freq_dev = response.shape[1]
     row_count = response.shape[2]
     focal_count = focus_plus.shape[3]
@@ -51,11 +60,9 @@
     local_onset = lax.dynamic_slice_in_dim(onset.reshape(-1), freq_index * piece_len, piece_len, 0)
     inverse, forward = make_tables(freq_dev * groups)
     shard_piece = lax.all_gather(focus_plus, "rec", axis=2, tiled=True)
-    real_block = response[0]
-    imag_block = response[1]
     joined = jnp.concatenate([shard_piece[0], shard_piece[1]], axis=2)
-    from_real = full_einsum("wrs,wsf->wrf", real_block, joined)
-    from_imag = full_einsum("wrs,wsf->wrf", imag_block, joined)
+    from_real = full_einsum("wrs,wsf->wrf", response[0], joined)
+    from_imag = full_einsum("wrs,wsf->wrf", response[1], joined)
     new_real = from_real[:, :, :focal_count] - from_imag[:, :, focal_count:]
     new_imag = from_real[:, :, focal_count:] + from_imag[:, :, :focal_count]
     spectra = jnp.stack([new_real, new_imag]).reshape(2, freq_dev, flat_count)
@@ -65,10 +72,8 @@
         2, freq_dev, row_count, focal_count
     )
     minus_joined = jnp.concatenate([focus_minus[0], focus_minus[1]], axis=2)
-    real_block = response[0]
-    imag_block = response[1]
-    from_real = full_einsum("wrs,wrf->swf", real_block, minus_joined)
-    from_imag = full_einsum("wrs,wrf->swf", imag_block, minus_joined)
+    from_real = full_einsum("wrs,wrf->swf", response[0], minus_joined)
+    from_imag = full_einsum("wrs,wrf->swf", response[1], minus_joined)
     h_real = from_real[:, :, :focal_count] + from_imag[:, :, focal_count:]
     h_imag = from_real[:, :, focal_count:] - from_imag[:, :, :focal_count]
     summed = lax.psum_scatter(
@@ -83,6 +88,388 @@
     return (focus_minus, direct + returned)
 
 
+def cas_tables(groups):
+    total = 2 * TILE * groups
+    order = np.array(
+        [g * 2 * TILE + half * TILE + k for half in range(2) for g in range(groups) for k in range(TILE)]
+    )
+    step = np.arange(total)[:, None] * order[None, :] % total
+    angle = step * (2.0 * math.pi / total)
+    into = np.cos(angle) + np.sin(angle)
+
+    def table(matrix):
+        hi = matrix.astype(ml_dtypes.bfloat16)
+        lo = (matrix - hi.astype(np.float64)).astype(ml_dtypes.bfloat16)
+        return np.concatenate(
+            [np.concatenate([hi, hi], 1), np.concatenate([lo, np.zeros_like(lo)], 1)], 0
+        )
+
+    return table(into), table(into.T / total)
+
+
+def split(value):
+    hi = value.astype(jnp.bfloat16)
+    lo = (value - hi.astype(jnp.float32)).astype(jnp.bfloat16)
+    return hi, lo
+
+
+def dot(left, right, left_dim, right_dim):
+    return lax.dot_general(
+        left, right, (((left_dim,), (right_dim,)), ((), ())), preferred_element_type=jnp.float32
+    )
+
+
+def kernel(
+    groups,
+    resp, plus, direct, onset, into, back,
+    minus_out, next_out,
+    gathered, rbuf, g_buf, x1, y_buf, fm, part, core_in, y_in, x2, upd,
+    ag_s, ag_r, own_sem, r_sem, a_s, a_r, rc_s, rc_r, ry_s, ry_r,
+):
+    me = lax.axis_index("freq")
+    rec = lax.axis_index("rec")
+    core = lax.rem(rec, 2)
+    sibling = rec + 1 - 2 * core
+    across = lax.rem(rec + 2, 4)
+    diagonal = lax.rem(sibling + 2, 4)
+    rows = resp.shape[2]
+    lane_parts = rows // 128
+    focal = plus.shape[2]
+    total = 2 * TILE * groups
+
+    barrier = pltpu.get_barrier_semaphore()
+    for d in range(1, groups):
+        pl.semaphore_signal(
+            barrier, inc=1, device_id=(lax.rem(me + d, groups), rec), device_id_type=MESH
+        )
+    for other in (sibling, across):
+        pl.semaphore_signal(barrier, inc=1, device_id=(me, other), device_id_type=MESH)
+
+    def response_copy(w, slot):
+        return pltpu.make_async_copy(resp.at[:, w], rbuf.at[slot], r_sem.at[slot])
+
+    for k in range(SLOTS):
+        response_copy(k, k).start()
+    pl.semaphore_wait(barrier, groups + 1)
+
+    def remote(src, dst, s_sem, d_sem, to):
+        return pltpu.make_async_remote_copy(
+            src_ref=src, dst_ref=dst, send_sem=s_sem, recv_sem=d_sem, device_id=to, device_id_type=MESH
+        )
+
+    def ag_copy(kind, half):
+        span = pl.ds(half * TILE, TILE)
+        if kind == 2:
+            return remote(
+                gathered.at[across, :, span], gathered.at[across, :, span],
+                ag_s.at[2, half], ag_r.at[2, half], (me, sibling),
+            )
+        return remote(
+            plus.at[:, span], gathered.at[rec, :, span],
+            ag_s.at[kind, half], ag_r.at[kind, half], (me, (across, sibling)[kind]),
+        )
+
+    def ag_landed(kind, half):
+        span = pl.ds(half * TILE, TILE)
+        slot = (across, sibling, diagonal)[kind]
+        place = gathered.at[slot, :, span]
+        return remote(
+            place, place, ag_s.at[kind, half], ag_r.at[kind, half], (me, (across, sibling, sibling)[kind])
+        )
+
+    def a2a_copies(phase, half, src, dst):
+        return [
+            remote(
+                src.at[half, :, :, peer], dst.at[half, :, :, me],
+                a_s.at[phase, d], a_r.at[phase, d], (peer, rec),
+            )
+            for d in range(1, groups)
+            for peer in (lax.rem(me + d, groups),)
+        ]
+
+    def a2a_own(phase, half, src, dst):
+        return pltpu.make_async_copy(src.at[half, :, :, me], dst.at[half, :, :, me], a_r.at[phase, 0])
+
+    def a2a_start(phase, half, src, dst):
+        for copy in a2a_copies(phase, half, src, dst):
+            copy.start()
+        a2a_own(phase, half, src, dst).start()
+
+    def a2a_sent(phase, half, src, dst):
+        for copy in a2a_copies(phase, half, src, dst):
+            copy.wait_send()
+
+    def a2a_landed(phase, half, src, dst):
+        a2a_own(phase, half, src, dst).wait()
+        for d in range(1, groups):
+            peer = lax.rem(me + groups - d, groups)
+            place = dst.at[half, :, :, peer]
+            remote(place, place, a_s.at[phase, d], a_r.at[phase, d], (peer, rec)).wait_recv()
+
+    def spread(dst, half, k, value):
+        for lh in range(lane_parts):
+            for c in range(2):
+                for grp in range(groups):
+                    at = (c * groups + grp) * TILE
+                    dst[half, lh, c, grp, pl.ds(k, TILE, stride=TILE), :] = value[
+                        at : at + TILE, lh * 128 : (lh + 1) * 128
+                    ]
+
+    def window(src, dst):
+        time = lax.broadcasted_iota(jnp.int32, (total, rows), 0)
+        distance = jnp.minimum(time, total - time)
+
+        def one(f, carry):
+            span = pl.ds(pl.multiple_of(f * TILE, TILE), TILE)
+            keep = distance < onset[me, pl.ds(f, 1), :]
+            for c in range(2):
+                block = jnp.concatenate(
+                    [
+                        jnp.concatenate(
+                            [src[half, lh, c, :, span, :].reshape(groups * TILE, 128) for half in range(2)], 0
+                        )
+                        for lh in range(lane_parts)
+                    ],
+                    1,
+                )
+                for step in range(2):
+                    hi, lo = split(block)
+                    both = dot((into, back)[step][...], jnp.concatenate([hi, lo], 0), 1, 0)
+                    block = both[:total] + both[total:]
+                    if step == 0:
+                        block = jnp.where(keep, block, 0.0)
+                for half in range(2):
+                    for lh in range(lane_parts):
+                        dst[half, lh, c, :, span, :] = block[
+                            half * groups * TILE : (half + 1) * groups * TILE, lh * 128 : (lh + 1) * 128
+                        ].reshape(groups, TILE, 128)
+            return carry
+
+        lax.fori_loop(0, TILE, one, 0)
+
+    own = pltpu.make_async_copy(plus, gathered.at[rec], own_sem)
+    own.start()
+    ag_copy(0, 0).start()
+    ag_copy(1, 0).start()
+    ag_copy(1, 1).start()
+    own.wait()
+
+    def g_step(half, k, carry):
+        w = half * TILE + k
+        slot = lax.rem(k, SLOTS)
+        response_copy(w, slot).wait()
+        plus_t = jnp.concatenate(
+            [jnp.concatenate([gathered[q, c, w] for q in range(4)], 1) for c in range(2)], 0
+        )
+        f_hi, f_lo = split(plus_t)
+        f_both = jnp.concatenate([f_hi, f_lo], 0)
+        products = []
+        for c in range(2):
+            hi, lo = split(rbuf[slot, c])
+            wide = dot(hi, f_both, 1, 1)
+            products.append(wide[:, : 2 * focal] + wide[:, 2 * focal :] + dot(lo, f_hi, 1, 1))
+        p_t, q_t = products[0].T, products[1].T
+        spread(g_buf, half, k, jnp.concatenate([p_t[:focal] - q_t[focal:], p_t[focal:] + q_t[:focal]], 0))
+        response_copy(lax.rem(w + SLOTS, 2 * TILE), slot).start()
+        return carry
+
+    for half in range(2):
+        ag_landed(0, half).wait_recv()
+        if half == 0:
+            ag_copy(0, 0).wait_send()
+            ag_copy(0, 1).start()
+        ag_copy(2, half).start()
+        ag_landed(1, half).wait_recv()
+        ag_landed(2, half).wait_recv()
+        lax.fori_loop(0, TILE, functools.partial(g_step, half), 0)
+        a2a_start(half, half, g_buf, x1)
+    for half in range(2):
+        a2a_landed(half, half, g_buf, x1)
+
+    window(x1, y_buf)
+
+    a2a_start(2, 0, y_buf, fm)
+    a2a_sent(2, 0, y_buf, fm)
+    a2a_start(3, 1, y_buf, fm)
+
+    def core_copy(half, yy):
+        return remote(
+            part.at[half, 2 * yy + 1 - core], core_in.at[half, yy],
+            rc_s.at[half, yy], rc_r.at[half, yy], (me, sibling),
+        )
+
+    def y_copy(half):
+        return remote(
+            part.at[half, across], y_in.at[half], ry_s.at[half], ry_r.at[half], (me, across)
+        )
+
+    def collect(src, half, k):
+        return jnp.concatenate(
+            [
+                jnp.concatenate(
+                    [
+                        src[half, lh, c, grp, pl.ds(k, TILE, stride=TILE), :]
+                        for c in range(2)
+                        for grp in range(groups)
+                    ],
+                    0,
+                )
+                for lh in range(lane_parts)
+            ],
+            1,
+        )
+
+    def h_step(half, k, carry):
+        w = half * TILE + k
+        slot = lax.rem(k, SLOTS)
+        minus_t = collect(fm, half, k)
+        for c in range(2):
+            minus_out[c, w] = minus_t[c * focal : (c + 1) * focal]
+        response_copy(w, slot).wait()
+        m_hi, m_lo = split(minus_t)
+        m_both = jnp.concatenate([m_hi, m_lo], 0)
+        for q in range(4):
+            products = []
+            for c in range(2):
+                hi, lo = split(rbuf[slot, c, :, q * rows : (q + 1) * rows])
+                wide = dot(m_both, hi, 1, 0)
+                products.append(wide[: 2 * focal] + wide[2 * focal :] + dot(m_hi, lo, 1, 0))
+            p_t, q_t = products
+            part[half, q, k] = jnp.concatenate([p_t[:focal] + q_t[focal:], p_t[focal:] - q_t[:focal]], 0)
+
+        if half == 0:
+            response_copy(w + SLOTS, slot).start()
+        else:
+
+            @pl.when(k < TILE - SLOTS)
+            def _():
+                response_copy(w + SLOTS, slot).start()
+
+        return carry
+
+    def core_sum(half):
+        y_mine = rec // 2
+        for yy in range(2):
+            core_copy(half, yy).start()
+        for yy in range(2):
+            core_copy(half, yy).wait_recv()
+
+        def add(k, carry):
+            part[half, across, k] = part[half, across, k] + core_in[half, 1 - y_mine, k]
+            return carry
+
+        lax.fori_loop(0, TILE, add, 0)
+        y_copy(half).start()
+
+    def y_sum(half):
+        y_mine = rec // 2
+        y_copy(half).wait_recv()
+
+        def add(k, carry):
+            spread(
+                g_buf, half, k, part[half, rec, k] + core_in[half, y_mine, k] + y_in[half, k]
+            )
+            return carry
+
+        lax.fori_loop(0, TILE, add, 0)
+        a2a_start(4 + half, half, g_buf, x2)
+
+    for half in range(2):
+        a2a_sent(half, half, g_buf, x1)
+    for half in range(2):
+        a2a_landed(2 + half, half, y_buf, fm)
+        lax.fori_loop(0, TILE, functools.partial(h_step, half), 0)
+        core_sum(half)
+        if half == 1:
+            y_sum(0)
+            y_sum(1)
+    a2a_sent(3, 1, y_buf, fm)
+    for half in range(2):
+        a2a_landed(4 + half, half, g_buf, x2)
+
+    window(x2, y_buf)
+
+    for half in range(2):
+        a2a_start(6 + half, half, y_buf, upd)
+
+    def final(half, k, carry):
+        w = half * TILE + k
+        value = collect(upd, half, k)
+        for c in range(2):
+            next_out[c, w] = direct[c, w] + value[c * focal : (c + 1) * focal]
+        return carry
+
+    for half in range(2):
+        a2a_landed(6 + half, half, y_buf, upd)
+        lax.fori_loop(0, TILE, functools.partial(final, half), 0)
+
+    for half in range(2):
+        a2a_sent(4 + half, half, g_buf, x2)
+        a2a_sent(6 + half, half, y_buf, upd)
+        ag_copy(1, half).wait_send()
+        ag_copy(2, half).wait_send()
+        y_copy(half).wait_send()
+        for yy in range(2):
+            core_copy(half, yy).wait_send()
+    ag_copy(0, 1).wait_send()
+
+
+def per_device_kernel(response, focus_plus, direct, onset):
+    groups = lax.axis_size("freq")
+    freq_dev, rows, positions = response.shape[1:]
+    focal = focus_plus.shape[3]
+    lane_parts = rows // 128
+    into, back = cas_tables(groups)
+    turned = (0, 1, 3, 2)
+    out = jax.ShapeDtypeStruct((2, freq_dev, focal, rows), jnp.float32)
+    traces = pltpu.VMEM((2, lane_parts, 2, groups, TILE * TILE, 128), jnp.float32)
+    vmem = pl.BlockSpec(memory_space=pltpu.VMEM)
+    anywhere = pl.BlockSpec(memory_space=pl.ANY)
+    dma = pltpu.SemaphoreType.DMA
+    minus, following = pl.pallas_call(
+        functools.partial(kernel, groups),
+        out_shape=(out, out),
+        in_specs=[anywhere, anywhere, vmem, vmem, vmem, vmem],
+        out_specs=(vmem, vmem),
+        scratch_shapes=[
+            pltpu.VMEM((4, 2, freq_dev, focal, rows), jnp.float32),
+            pltpu.VMEM((SLOTS, 2, rows, positions), jnp.float32),
+            traces, traces, traces, traces,
+            pltpu.VMEM((2, 4, TILE, 2 * focal, rows), jnp.float32),
+            pltpu.VMEM((2, 2, TILE, 2 * focal, rows), jnp.float32),
+            pltpu.VMEM((2, TILE, 2 * focal, rows), jnp.float32),
+            traces, traces,
+            dma((3, 2)), dma((3, 2)), dma, dma((SLOTS,)),
+            dma((8, groups)), dma((8, groups)),
+            dma((2, 2)), dma((2, 2)), dma((2,)), dma((2,)),
+        ],
+        compiler_params=pltpu.CompilerParams(
+            collective_id=0, has_side_effects=True, vmem_limit_bytes=61 * 1024 * 1024
+        ),
+    )(
+        response,
+        jnp.transpose(focus_plus, turned),
+        jnp.transpose(direct, turned),
+        onset.T.reshape(groups, TILE, rows),
+        jnp.asarray(into),
+        jnp.asarray(back),
+    )
+    return jnp.transpose(minus, turned), jnp.transpose(following, turned)
+
+
+def per_device(response, focus_plus, direct, onset):
+    freq_dev, rows, positions = response.shape[1:]
+    fits = (
+        lax.axis_size("rec") == 4
+        and positions == 4 * rows
+        and rows % 128 == 0
+        and freq_dev == 2 * TILE
+        and focus_plus.shape[3] == TILE * lax.axis_size("freq")
+    )
+    form = per_device_kernel if fits else per_device_general
+    return form(response, focus_plus, direct, onset)
+
+
 def solution(mesh):
     placed = (
         P(None, "freq", "rec", None),

time: 720 us -> 258 us (0.36); the launches traced: 707 us -> 258 us
  Pallas kernels: 0 us -> 253 us
  local copies, waits for them, and re-layouts: 240 us -> 4.6 us
  waiting for transfers between devices: 209 us -> 0 us
  blocking collectives: 102 us -> 0 us
  matrix products: 81.8 us -> 0 us
  other arithmetic: 45.9 us -> 0 us
  between operations: 14.7 us -> 0.65 us
  starting transfers between devices: 12.9 us -> 0 us
    pallas_call x0 -> x1, Pallas kernels: none -> 253 us  [per_device_kernel(): pl.pallas_call(functools.partial(kernel, groups), out_shape=(out, out), i...]
    unnamed x22 -> x4, local copies, waits for them, and re-layouts: 122 us -> 4.6 us
    all_to_all x2 -> x0, blocking collectives: 102 us -> none  [the longest x1 51.6 us: per_device(): lax.all_to_all(filtered, 'freq', split_axis=1, concat_axis=2, tiled=True)]
    dot_general x8 -> x0, matrix products: 81.8 us -> none  [the longest x4 72.3 us: full_einsum(): return jnp.einsum(form, left, right, precision=lax.Precision.HIGHEST)]
    all_to_all x2 -> x0, waiting for transfers between devices: 74.9 us -> none  [the longest x1 44.2 us: per_device(): lax.all_to_all(spectra, 'freq', split_axis=2, concat_axis=1, tiled=True)]
    reduce_scatter x1 -> x0, waiting for transfers between devices: 73 us -> none  [per_device(): lax.psum_scatter(jnp.stack([h_real, h_imag], axis=1), 'rec', scatter_dime...]
    all_gather x1 -> x0, waiting for transfers between devices: 60.6 us -> none  [per_device(): shard_piece = lax.all_gather(focus_plus, 'rec', axis=2, tiled=True)]
    all_to_all x7 -> x0, local copies, waits for them, and re-layouts: 50 us -> none  [the longest x1 21.6 us: per_device(): lax.all_to_all(arranged_sum, 'freq', split_axis=2, concat_axis=1, tiled=T...]
  transfers between devices with their start and end apart: 4 -> 0, of which waited for: 4 -> 0; matrix products, arithmetic and copies ran while one was open for 2% -> 0% of each run, Pallas kernels for 0% -> 0%
where the time goes in v1:
time: 258 us
  Pallas kernels  253 us (98%)
  local copies, waits for them, and re-layouts  4.6 us (2%)
    pallas_call x1, Pallas kernels, per_device_kernel(): pl.pallas_call(functools.partial(kernel, groups), out_shape=(out, out), i...  253 us

profile of v1, /device:TPU:15, one launch (start us, length us, event | category | flops | bytes accessed | tf_op | source)
XLA Modules:
  0.0 258.1 jit_solution(17404071266712772139)
XLA Ops:
  0.6 252.9 %shard_map.77 = (f32[2,16,64,256]{3,2,1,0:T(8,128)}, f32[2,16,64,256]{3,2,1,0:T(8,128)}) custom-call(f32[2,16,256,1024]{3,2,1,0:T(8,128)} %resp.1, f32[2,16,64,256]{3,2,1,0:T(8,128)} %bitcast.7, f32[2,16,64,256]{3,2,1,0:T(8,128)} %bitcast.8, s32[8,8,256]{2,1,0:T(8,128)} %bitcast.11, bf16[256,256]{1,0:T(8,128)(2,1)} %constant.4.clone.into, ...), custom_call_target="tpu_custom_call" | custom-call | tf_op jit(solution)/shard_map/pallas_call | solution.py:429
  253.5 0.0 copy-start
  253.5 3.3 %copy.10 = f32[2,16,256,64]{2,3,1,0:T(8,128)} copy(f32[2,16,256,64]{2,3,1,0:T(8,128)} %bitcast.10) | data formatting | bytes 4194304
  256.8 0.0 copy-done
  256.8 1.3 copy.11
Async XLA Ops:
  253.5 3.3 %copy-start = (f32[2,16,64,256]{3,2,1,0:T(8,128)S(1)}, f32[2,16,64,256]{3,2,1,0:T(8,128)}, u32[]{:S(2)}) copy-start(f32[2,16,64,256]{3,2,1,0:T(8,128)} %get-tuple-element.5) | copy-start | bytes 6291460

commit v2 on v1

--- a/solution.py
+++ b/solution.py
@@ -12,7 +12,10 @@
 
 MESH = pl.DeviceIdType.MESH
 SLOTS = 4
-TILE = 8
+GROUP = 8
+PARTS = 4
+PART = 4
+PAIR = 2
 
 
 def full_einsum(form, left, right):
@@ -89,20 +92,22 @@
 
 
 def cas_tables(groups):
-    total = 2 * TILE * groups
-    order = np.array(
-        [g * 2 * TILE + half * TILE + k for half in range(2) for g in range(groups) for k in range(TILE)]
-    )
-    step = np.arange(total)[:, None] * order[None, :] % total
-    angle = step * (2.0 * math.pi / total)
-    into = np.cos(angle) + np.sin(angle)
+    per = PARTS * PART
+    total = per * groups
+    freq = np.array(
+        [
+            (f, g * per + q * PART + k)
+            for q in range(PARTS) for g in range(groups) for f in range(PAIR) for k in range(PART)
+        ]
+    )
+    time = np.array([(f, t) for f in range(PAIR) for t in range(total)])
+    angle = time[:, None, 1] * freq[None, :, 1] % total * (2.0 * math.pi / total)
+    into = np.where(time[:, None, 0] == freq[None, :, 0], np.cos(angle) + np.sin(angle), 0.0)
 
     def table(matrix):
         hi = matrix.astype(ml_dtypes.bfloat16)
         lo = (matrix - hi.astype(np.float64)).astype(ml_dtypes.bfloat16)
-        return np.concatenate(
-            [np.concatenate([hi, hi], 1), np.concatenate([lo, np.zeros_like(lo)], 1)], 0
-        )
+        return np.concatenate([hi, lo], 0)
 
     return table(into), table(into.T / total)
 
@@ -135,7 +140,7 @@
     rows = resp.shape[2]
     lane_parts = rows // 128
     focal = plus.shape[2]
-    total = 2 * TILE * groups
+    total = PARTS * PART * groups
 
     barrier = pltpu.get_barrier_semaphore()
     for d in range(1, groups):
@@ -158,7 +163,7 @@
         )
 
     def ag_copy(kind, half):
-        span = pl.ds(half * TILE, TILE)
+        span = pl.ds(half * PART, PART)
         if kind == 2:
             return remote(
                 gathered.at[across, :, span], gathered.at[across, :, span],
@@ -170,93 +175,115 @@
         )
 
     def ag_landed(kind, half):
-        span = pl.ds(half * TILE, TILE)
+        span = pl.ds(half * PART, PART)
         slot = (across, sibling, diagonal)[kind]
         place = gathered.at[slot, :, span]
         return remote(
             place, place, ag_s.at[kind, half], ag_r.at[kind, half], (me, (across, sibling, sibling)[kind])
         )
 
-    def a2a_copies(phase, half, src, dst):
+    def a2a_peers(phase, src, dst, pick):
         return [
-            remote(
-                src.at[half, :, :, peer], dst.at[half, :, :, me],
-                a_s.at[phase, d], a_r.at[phase, d], (peer, rec),
-            )
+            remote(pick(src, peer), pick(dst, me), a_s.at[phase, d], a_r.at[phase, d], (peer, rec))
             for d in range(1, groups)
             for peer in (lax.rem(me + d, groups),)
         ]
 
-    def a2a_own(phase, half, src, dst):
-        return pltpu.make_async_copy(src.at[half, :, :, me], dst.at[half, :, :, me], a_r.at[phase, 0])
-
-    def a2a_start(phase, half, src, dst):
-        for copy in a2a_copies(phase, half, src, dst):
+    def a2a_begin(phase, src, dst, pick):
+        for copy in a2a_peers(phase, src, dst, pick):
             copy.start()
-        a2a_own(phase, half, src, dst).start()
-
-    def a2a_sent(phase, half, src, dst):
-        for copy in a2a_copies(phase, half, src, dst):
+        pltpu.make_async_copy(pick(src, me), pick(dst, me), a_r.at[phase, 0]).start()
+
+    def a2a_left(phase, src, dst, pick):
+        for copy in a2a_peers(phase, src, dst, pick):
             copy.wait_send()
 
-    def a2a_landed(phase, half, src, dst):
-        a2a_own(phase, half, src, dst).wait()
+    def a2a_arrived(phase, src, dst, pick):
+        pltpu.make_async_copy(pick(src, me), pick(dst, me), a_r.at[phase, 0]).wait()
         for d in range(1, groups):
             peer = lax.rem(me + groups - d, groups)
-            place = dst.at[half, :, :, peer]
+            place = pick(dst, peer)
             remote(place, place, a_s.at[phase, d], a_r.at[phase, d], (peer, rec)).wait_recv()
+
+    def of_part(q):
+        return lambda ref, place: ref.at[q, :, :, place]
+
+    def of_real(c):
+        return lambda ref, place: ref.at[:, :, c, place]
+
+    def a2a_start(phase, q, src, dst):
+        a2a_begin(phase, src, dst, of_part(q))
+
+    def a2a_sent(phase, q, src, dst):
+        a2a_left(phase, src, dst, of_part(q))
+
+    def a2a_landed(phase, q, src, dst):
+        a2a_arrived(phase, src, dst, of_part(q))
+
+    def last_start(c):
+        a2a_begin(3 * PARTS + c, y_buf, upd, of_real(c))
+
+    def last_sent(c):
+        a2a_left(3 * PARTS + c, y_buf, upd, of_real(c))
+
+    def last_landed(c):
+        a2a_arrived(3 * PARTS + c, y_buf, upd, of_real(c))
 
     def spread(dst, half, k, value):
         for lh in range(lane_parts):
             for c in range(2):
                 for grp in range(groups):
-                    at = (c * groups + grp) * TILE
-                    dst[half, lh, c, grp, pl.ds(k, TILE, stride=TILE), :] = value[
-                        at : at + TILE, lh * 128 : (lh + 1) * 128
+                    at = (c * groups + grp) * GROUP
+                    dst[half, lh, c, grp, pl.ds(k, GROUP, stride=PART), :] = value[
+                        at : at + GROUP, lh * 128 : (lh + 1) * 128
                     ]
 
-    def window(src, dst):
-        time = lax.broadcasted_iota(jnp.int32, (total, rows), 0)
+    def window(src, dst, c):
+        row = lax.broadcasted_iota(jnp.int32, (PAIR * total, rows), 0)
+        time = lax.rem(row, total)
         distance = jnp.minimum(time, total - time)
+        tall = groups * PAIR * PART
 
         def one(f, carry):
-            span = pl.ds(pl.multiple_of(f * TILE, TILE), TILE)
-            keep = distance < onset[me, pl.ds(f, 1), :]
-            for c in range(2):
-                block = jnp.concatenate(
-                    [
-                        jnp.concatenate(
-                            [src[half, lh, c, :, span, :].reshape(groups * TILE, 128) for half in range(2)], 0
-                        )
-                        for lh in range(lane_parts)
-                    ],
-                    1,
-                )
-                for step in range(2):
-                    hi, lo = split(block)
-                    both = dot((into, back)[step][...], jnp.concatenate([hi, lo], 0), 1, 0)
-                    block = both[:total] + both[total:]
-                    if step == 0:
-                        block = jnp.where(keep, block, 0.0)
-                for half in range(2):
-                    for lh in range(lane_parts):
-                        dst[half, lh, c, :, span, :] = block[
-                            half * groups * TILE : (half + 1) * groups * TILE, lh * 128 : (lh + 1) * 128
-                        ].reshape(groups, TILE, 128)
+            span = pl.ds(pl.multiple_of(f * PAIR * PART, PAIR * PART), PAIR * PART)
+            first = onset[me, pl.ds(PAIR * f, 1), :]
+            second = onset[me, pl.ds(PAIR * f + 1, 1), :]
+            keep = distance < jnp.where(row < total, first, second)
+            block = jnp.concatenate(
+                [
+                    jnp.concatenate(
+                        [src[q, lh, c, :, span, :].reshape(tall, 128) for q in range(PARTS)], 0
+                    )
+                    for lh in range(lane_parts)
+                ],
+                1,
+            )
+            for step in range(2):
+                hi, lo = split(block)
+                table = (into, back)[step]
+                both = dot(table[...], hi, 1, 0)
+                block = both[: PAIR * total] + both[PAIR * total :] + dot(table[: PAIR * total], lo, 1, 0)
+                if step == 0:
+                    block = jnp.where(keep, block, 0.0)
+            for q in range(PARTS):
+                for lh in range(lane_parts):
+                    dst[q, lh, c, :, span, :] = block[
+                        q * tall : (q + 1) * tall, lh * 128 : (lh + 1) * 128
+                    ].reshape(groups, PAIR * PART, 128)
             return carry
 
-        lax.fori_loop(0, TILE, one, 0)
+        lax.fori_loop(0, GROUP // PAIR, one, 0)
 
     own = pltpu.make_async_copy(plus, gathered.at[rec], own_sem)
+    ag_copy(0, 0).start()
     own.start()
-    ag_copy(0, 0).start()
-    ag_copy(1, 0).start()
-    ag_copy(1, 1).start()
+    for part_no in range(PARTS):
+        ag_copy(1, part_no).start()
     own.wait()
 
     def g_step(half, k, carry):
-        w = half * TILE + k
-        slot = lax.rem(k, SLOTS)
+        w = half * PART + k
+        slot = lax.rem(w, SLOTS)
         response_copy(w, slot).wait()
         plus_t = jnp.concatenate(
             [jnp.concatenate([gathered[q, c, w] for q in range(4)], 1) for c in range(2)], 0
@@ -270,27 +297,29 @@
             products.append(wide[:, : 2 * focal] + wide[:, 2 * focal :] + dot(lo, f_hi, 1, 1))
         p_t, q_t = products[0].T, products[1].T
         spread(g_buf, half, k, jnp.concatenate([p_t[:focal] - q_t[focal:], p_t[focal:] + q_t[:focal]], 0))
-        response_copy(lax.rem(w + SLOTS, 2 * TILE), slot).start()
+        response_copy(lax.rem(w + SLOTS, PARTS * PART), slot).start()
         return carry
 
-    for half in range(2):
+    for half in range(PARTS):
         ag_landed(0, half).wait_recv()
         if half == 0:
             ag_copy(0, 0).wait_send()
             ag_copy(0, 1).start()
+        if half + 2 < PARTS:
+            ag_copy(0, half + 2).start()
         ag_copy(2, half).start()
         ag_landed(1, half).wait_recv()
         ag_landed(2, half).wait_recv()
-        lax.fori_loop(0, TILE, functools.partial(g_step, half), 0)
+        lax.fori_loop(0, PART, functools.partial(g_step, half), 0)
         a2a_start(half, half, g_buf, x1)
-    for half in range(2):
+    for half in range(PARTS):
         a2a_landed(half, half, g_buf, x1)
 
-    window(x1, y_buf)
-
-    a2a_start(2, 0, y_buf, fm)
-    a2a_sent(2, 0, y_buf, fm)
-    a2a_start(3, 1, y_buf, fm)
+    window(x1, y_buf, 0)
+    window(x1, y_buf, 1)
+
+    a2a_start(PARTS, 0, y_buf, fm)
+    a2a_start(PARTS + 1, 1, y_buf, fm)
 
     def core_copy(half, yy):
         return remote(
@@ -303,13 +332,13 @@
             part.at[half, across], y_in.at[half], ry_s.at[half], ry_r.at[half], (me, across)
         )
 
-    def collect(src, half, k):
+    def collect(src, half, k, parts):
         return jnp.concatenate(
             [
                 jnp.concatenate(
                     [
-                        src[half, lh, c, grp, pl.ds(k, TILE, stride=TILE), :]
-                        for c in range(2)
+                        src[half, lh, c, grp, pl.ds(k, GROUP, stride=PART), :]
+                        for c in parts
                         for grp in range(groups)
                     ],
                     0,
@@ -320,9 +349,9 @@
         )
 
     def h_step(half, k, carry):
-        w = half * TILE + k
-        slot = lax.rem(k, SLOTS)
-        minus_t = collect(fm, half, k)
+        w = half * PART + k
+        slot = lax.rem(w, SLOTS)
+        minus_t = collect(fm, half, k, (0, 1))
         for c in range(2):
             minus_out[c, w] = minus_t[c * focal : (c + 1) * focal]
         response_copy(w, slot).wait()
@@ -337,13 +366,9 @@
             p_t, q_t = products
             part[half, q, k] = jnp.concatenate([p_t[:focal] + q_t[focal:], p_t[focal:] - q_t[:focal]], 0)
 
-        if half == 0:
+        @pl.when(w + SLOTS < PARTS * PART)
+        def _():
             response_copy(w + SLOTS, slot).start()
-        else:
-
-            @pl.when(k < TILE - SLOTS)
-            def _():
-                response_copy(w + SLOTS, slot).start()
 
         return carry
 
@@ -358,7 +383,7 @@
             part[half, across, k] = part[half, across, k] + core_in[half, 1 - y_mine, k]
             return carry
 
-        lax.fori_loop(0, TILE, add, 0)
+        lax.fori_loop(0, PART, add, 0)
         y_copy(half).start()
 
     def y_sum(half):
@@ -371,47 +396,50 @@
             )
             return carry
 
-        lax.fori_loop(0, TILE, add, 0)
-        a2a_start(4 + half, half, g_buf, x2)
-
-    for half in range(2):
+        lax.fori_loop(0, PART, add, 0)
+        a2a_start(2 * PARTS + half, half, g_buf, x2)
+
+    for half in range(PARTS):
         a2a_sent(half, half, g_buf, x1)
-    for half in range(2):
-        a2a_landed(2 + half, half, y_buf, fm)
-        lax.fori_loop(0, TILE, functools.partial(h_step, half), 0)
+    for half in range(PARTS):
+        if half + 2 < PARTS:
+            a2a_sent(PARTS + half, half, y_buf, fm)
+            a2a_start(PARTS + half + 2, half + 2, y_buf, fm)
+        a2a_landed(PARTS + half, half, y_buf, fm)
+        lax.fori_loop(0, PART, functools.partial(h_step, half), 0)
         core_sum(half)
-        if half == 1:
-            y_sum(0)
-            y_sum(1)
-    a2a_sent(3, 1, y_buf, fm)
-    for half in range(2):
-        a2a_landed(4 + half, half, g_buf, x2)
-
-    window(x2, y_buf)
-
-    for half in range(2):
-        a2a_start(6 + half, half, y_buf, upd)
-
-    def final(half, k, carry):
-        w = half * TILE + k
-        value = collect(upd, half, k)
-        for c in range(2):
-            next_out[c, w] = direct[c, w] + value[c * focal : (c + 1) * focal]
+        if half > 0:
+            y_sum(half - 1)
+    y_sum(PARTS - 1)
+    for half in range(PARTS - 2, PARTS):
+        a2a_sent(PARTS + half, half, y_buf, fm)
+    for half in range(PARTS):
+        a2a_landed(2 * PARTS + half, half, g_buf, x2)
+
+    for c in range(2):
+        window(x2, y_buf, c)
+        last_start(c)
+
+    def final(c, w, carry):
+        value = collect(upd, w // PART, lax.rem(w, PART), (c,))
+        next_out[c, w] = direct[c, w] + value
         return carry
 
-    for half in range(2):
-        a2a_landed(6 + half, half, y_buf, upd)
-        lax.fori_loop(0, TILE, functools.partial(final, half), 0)
-
-    for half in range(2):
-        a2a_sent(4 + half, half, g_buf, x2)
-        a2a_sent(6 + half, half, y_buf, upd)
+    for c in range(2):
+        last_landed(c)
+        lax.fori_loop(0, PARTS * PART, functools.partial(final, c), 0)
+
+    for c in range(2):
+        last_sent(c)
+    for half in range(PARTS):
+        a2a_sent(2 * PARTS + half, half, g_buf, x2)
+        if half > 0:
+            ag_copy(0, half).wait_send()
         ag_copy(1, half).wait_send()
         ag_copy(2, half).wait_send()
         y_copy(half).wait_send()
         for yy in range(2):
             core_copy(half, yy).wait_send()
-    ag_copy(0, 1).wait_send()
 
 
 def per_device_kernel(response, focus_plus, direct, onset):
@@ -422,7 +450,7 @@
     into, back = cas_tables(groups)
     turned = (0, 1, 3, 2)
     out = jax.ShapeDtypeStruct((2, freq_dev, focal, rows), jnp.float32)
-    traces = pltpu.VMEM((2, lane_parts, 2, groups, TILE * TILE, 128), jnp.float32)
+    traces = pltpu.VMEM((PARTS, lane_parts, 2, groups, GROUP * PART, 128), jnp.float32)
     vmem = pl.BlockSpec(memory_space=pltpu.VMEM)
     anywhere = pl.BlockSpec(memory_space=pl.ANY)
     dma = pltpu.SemaphoreType.DMA
@@ -435,13 +463,13 @@
             pltpu.VMEM((4, 2, freq_dev, focal, rows), jnp.float32),
             pltpu.VMEM((SLOTS, 2, rows, positions), jnp.float32),
             traces, traces, traces, traces,
-            pltpu.VMEM((2, 4, TILE, 2 * focal, rows), jnp.float32),
-            pltpu.VMEM((2, 2, TILE, 2 * focal, rows), jnp.float32),
-            pltpu.VMEM((2, TILE, 2 * focal, rows), jnp.float32),
+            pltpu.VMEM((PARTS, 4, PART, 2 * focal, rows), jnp.float32),
+            pltpu.VMEM((PARTS, 2, PART, 2 * focal, rows), jnp.float32),
+            pltpu.VMEM((PARTS, PART, 2 * focal, rows), jnp.float32),
             traces, traces,
-            dma((3, 2)), dma((3, 2)), dma, dma((SLOTS,)),
-            dma((8, groups)), dma((8, groups)),
-            dma((2, 2)), dma((2, 2)), dma((2,)), dma((2,)),
+            dma((3, PARTS)), dma((3, PARTS)), dma, dma((SLOTS,)),
+            dma((3 * PARTS + 2, groups)), dma((3 * PARTS + 2, groups)),
+            dma((PARTS, 2)), dma((PARTS, 2)), dma((PARTS,)), dma((PARTS,)),
         ],
         compiler_params=pltpu.CompilerParams(
             collective_id=0, has_side_effects=True, vmem_limit_bytes=61 * 1024 * 1024
@@ -450,7 +478,7 @@
         response,
         jnp.transpose(focus_plus, turned),
         jnp.transpose(direct, turned),
-        onset.T.reshape(groups, TILE, rows),
+        onset.T.reshape(groups, GROUP, rows),
         jnp.asarray(into),
         jnp.asarray(back),
     )
@@ -463,8 +491,8 @@
         lax.axis_size("rec") == 4
         and positions == 4 * rows
         and rows % 128 == 0
-        and freq_dev == 2 * TILE
-        and focus_plus.shape[3] == TILE * lax.axis_size("freq")
+        and freq_dev == PARTS * PART
+        and focus_plus.shape[3] == GROUP * lax.axis_size("freq")
     )
     form = per_device_kernel if fits else per_device_general
     return form(response, focus_plus, direct, onset)

time: 258 us -> 229 us (0.89)
  Pallas kernels: 253 us -> 223 us
    pallas_call x1, Pallas kernels: 253 us -> 223 us  [per_device_kernel(): pl.pallas_call(functools.partial(kernel, groups), out_shape=(out, out), i...]
where the time goes in v2:
time: 229 us; the launch traced here: 228 us
  Pallas kernels  223 us (97%)
  local copies, waits for them, and re-layouts  4.6 us (2%)
    pallas_call x1, Pallas kernels, per_device_kernel(): pl.pallas_call(functools.partial(kernel, groups), out_shape=(out, out), i...  223 us
    unnamed x4, local copies, waits for them, and re-layouts  4.6 us

profile of v2, /device:TPU:15, one launch (start us, length us, event | category | flops | bytes accessed | tf_op | source)
XLA Modules:
  0.0 228.0 jit_solution(34793362841313491)
XLA Ops:
  0.6 222.7 %shard_map.77 = (f32[2,16,64,256]{3,2,1,0:T(8,128)}, f32[2,16,64,256]{3,2,1,0:T(8,128)}) custom-call(f32[2,16,256,1024]{3,2,1,0:T(8,128)} %resp.1, f32[2,16,64,256]{3,2,1,0:T(8,128)} %bitcast.7, f32[2,16,64,256]{3,2,1,0:T(8,128)} %bitcast.8, s32[8,8,256]{2,1,0:T(8,128)} %bitcast.11, bf16[512,256]{1,0:T(8,128)(2,1)} %constant.4.clone.into, ...), custom_call_target="tpu_custom_call" | custom-call | tf_op jit(solution)/shard_map/pallas_call | solution.py:457
  223.3 0.0 copy-start
  223.4 3.3 %copy.10 = f32[2,16,256,64]{2,3,1,0:T(8,128)} copy(f32[2,16,256,64]{2,3,1,0:T(8,128)} %bitcast.10) | data formatting | bytes 4194304
  226.6 0.0 copy-done
  226.6 1.3 copy.11
Async XLA Ops:
  223.3 3.3 %copy-start = (f32[2,16,64,256]{3,2,1,0:T(8,128)S(1)}, f32[2,16,64,256]{3,2,1,0:T(8,128)}, u32[]{:S(2)}) copy-start(f32[2,16,64,256]{3,2,1,0:T(8,128)} %get-tuple-element.5) | copy-start | bytes 6291460

commit v3 on v2

--- a/solution.py
+++ b/solution.py
@@ -185,7 +185,7 @@
     def a2a_peers(phase, src, dst, pick):
         return [
             remote(pick(src, peer), pick(dst, me), a_s.at[phase, d], a_r.at[phase, d], (peer, rec))
-            for d in range(1, groups)
+            for d in sorted(range(1, groups), key=lambda d: -abs(2 * d - groups))
             for peer in (lax.rem(me + d, groups),)
         ]
 

time: 229 us -> 226 us (0.987)
  the two profiles are of different devices: /device:TPU:15 before, /device:TPU:6 now
where the time goes in v3:
time: 226 us; the launch traced here: 225 us
  Pallas kernels  220 us (97%)
  local copies, waits for them, and re-layouts  4.6 us (2%)
    pallas_call x1, Pallas kernels, per_device_kernel(): pl.pallas_call(functools.partial(kernel, groups), out_shape=(out, out), i...  220 us
    unnamed x4, local copies, waits for them, and re-layouts  4.6 us

profile of v3, /device:TPU:6, one launch (start us, length us, event | category | flops | bytes accessed | tf_op | source)
XLA Modules:
  0.0 225.5 jit_solution(2714815332585908367)
XLA Ops:
  0.6 220.2 %shard_map.77 = (f32[2,16,64,256]{3,2,1,0:T(8,128)}, f32[2,16,64,256]{3,2,1,0:T(8,128)}) custom-call(f32[2,16,256,1024]{3,2,1,0:T(8,128)} %resp.1, f32[2,16,64,256]{3,2,1,0:T(8,128)} %bitcast.7, f32[2,16,64,256]{3,2,1,0:T(8,128)} %bitcast.8, s32[8,8,256]{2,1,0:T(8,128)} %bitcast.11, bf16[512,256]{1,0:T(8,128)(2,1)} %constant.4.clone.into, ...), custom_call_target="tpu_custom_call" | custom-call | tf_op jit(solution)/shard_map/pallas_call | solution.py:457
  220.9 0.0 copy-start
  220.9 3.3 %copy.10 = f32[2,16,256,64]{2,3,1,0:T(8,128)} copy(f32[2,16,256,64]{2,3,1,0:T(8,128)} %bitcast.10) | data formatting | bytes 4194304
  224.2 0.0 copy-done
  224.2 1.3 copy.11
Async XLA Ops:
  220.9 3.3 %copy-start = (f32[2,16,64,256]{3,2,1,0:T(8,128)S(1)}, f32[2,16,64,256]{3,2,1,0:T(8,128)}, u32[]{:S(2)}) copy-start(f32[2,16,64,256]{3,2,1,0:T(8,128)} %get-tuple-element.5) | copy-start | bytes 6291460
